TPU v7x, 32 devices: a whole 2x2x4 slice. The times are simulated.
32 devices in a mesh: dp: 2 (over core), fsdp: 16 (over z, y, x).
Axes of the slice: x: 2, y: 2, z: 4, core: 2. Of those that a mesh axis runs over, the one named last changes fastest.
Arguments:
- tokens: bfloat16 [64, 392, 768], P(('dp', 'fsdp')), may hold values from -6 to 6
- positions: int32 [64, 392], P(('dp', 'fsdp')), may hold values from 0 to 1567, as said below
- counts: int32 [64], P(('dp', 'fsdp')), may hold values from 78 to 392, as said below
- cotangent: bfloat16 [64, 392, 768], P(('dp', 'fsdp')), may hold values from -6 to 6
- qkv_weight: float32 [768, 2304], P('fsdp'), may hold values from -0.21875 to 0.21875
- out_weight: float32 [768, 768], P('fsdp'), may hold values from -3.5 to 3.5
- up_weight: float32 [768, 3072], P('fsdp'), may hold values from -0.21875 to 0.21875
- down_weight: float32 [3072, 768], P('fsdp'), may hold values from -0.109375 to 0.109375
- small_params: float32 [768, 12], P('fsdp'), may hold values from -2 to 2
- qkv_momentum: float32 [768, 2304], P('fsdp'), may hold values from -256 to 256
- out_momentum: float32 [768, 768], P('fsdp'), may hold values from -48 to 48
- up_momentum: float32 [768, 3072], P('fsdp'), may hold values from -384 to 384
- down_momentum: float32 [3072, 768], P('fsdp'), may hold values from -384 to 384
- small_momentum: float32 [768, 12], P('fsdp'), may hold values from -512 to 512
- qkv_average: float32 [768, 2304], P('fsdp'), may hold values from -0.21875 to 0.21875
- out_average: float32 [768, 768], P('fsdp'), may hold values from -3.5 to 3.5
- up_average: float32 [768, 3072], P('fsdp'), may hold values from -0.21875 to 0.21875
- down_average: float32 [3072, 768], P('fsdp'), may hold values from -0.109375 to 0.109375
- small_average: float32 [768, 12], P('fsdp'), may hold values from -6 to 6
Outputs:
- block_out: bfloat16 [64, 392, 768], P(('dp', 'fsdp'))
- token_grad: float32 [64, 392, 768], P(('dp', 'fsdp'))
- new_qkv_weight: float32 [768, 2304], P('fsdp')
- new_out_weight: float32 [768, 768], P('fsdp')
- new_up_weight: float32 [768, 3072], P('fsdp')
- new_down_weight: float32 [3072, 768], P('fsdp')
- new_small_params: float32 [768, 12], P('fsdp')
- new_qkv_momentum: float32 [768, 2304], P('fsdp')
- new_out_momentum: float32 [768, 768], P('fsdp')
- new_up_momentum: float32 [768, 3072], P('fsdp')
- new_down_momentum: float32 [3072, 768], P('fsdp')
- new_small_momentum: float32 [768, 12], P('fsdp')
- new_qkv_average: float32 [768, 2304], P('fsdp')
- new_out_average: float32 [768, 768], P('fsdp')
- new_up_average: float32 [768, 3072], P('fsdp')
- new_down_average: float32 [3072, 768], P('fsdp')
- new_small_average: float32 [768, 12], P('fsdp')
- norms: float32 [10], replicated
Inputs may be any that keep to these rules, and one draw needn't show every extreme that they name: `counts`: some clip has exactly 392 visible tubelets and some exactly 78. The 392 positions of a clip are distinct; rows at and after a clip's count are padding.
All inputs are finite; a program needn't handle non-finite values.
Results may differ from a plain program's by a relative error of at most 0.012.
The roundings to bfloat16 on the way count: a program that leaves them out, or rounds other values in their place, can miss the bound.
Values may be sent and summed in bfloat16 or wider, within the bound.
No kernel may reach another device: no remote copies, remote signals or barrier semaphores. Data moves between devices by JAX's collectives and lax.ppermute only.
A program may use at most 256 MiB of HBM per device.

v0:
```python
import math
import jax
import jax.numpy as jnp
from jax import lax
from jax.sharding import PartitionSpec as P

HEAD_DIM = 64
EPS_NORM = 1e-06
MOMENTUM_DECAY = 0.9
WEIGHT_DECAY = 0.0001
TRUST_RATE = 0.2
AVERAGE_DECAY = 0.8


def sinusoid(positions, width):
    half_width = width // 2
    freqs = jnp.exp(jnp.arange(half_width, dtype=jnp.float32) * (-2.0 * math.log(10000.0) / width))
    angles = positions.astype(jnp.float32)[..., None] * freqs
    return jnp.stack([jnp.sin(angles), jnp.cos(angles)], axis=-1).reshape(
        positions.shape + (width,)
    )


def normalize(values):
    center = values - jnp.mean(values, axis=-1, keepdims=True)
    inv_std = lax.rsqrt(jnp.mean(center * center, axis=-1, keepdims=True) + EPS_NORM)
    return (center * inv_std, inv_std)


def norm_back(grad_hat, normed, inv_std):
    first_mean = jnp.mean(grad_hat, axis=-1, keepdims=True)
    second_mean = jnp.mean(grad_hat * normed, axis=-1, keepdims=True)
    return inv_std * (grad_hat - first_mean - normed * second_mean)


def split_small(small_low):
    pieces = [small_low[:, i].astype(jnp.float32) for i in range(8)]
    return (pieces, small_low[:, 8:].astype(jnp.float32).reshape(-1))


def update_group(weight, grad, moment, average, grad_norm, weight_norm):
    effective = grad + WEIGHT_DECAY * weight
    moment_new = MOMENTUM_DECAY * moment + effective
    rate = TRUST_RATE * weight_norm / (grad_norm + WEIGHT_DECAY * weight_norm)
    weight_new = weight - rate * (effective + MOMENTUM_DECAY * moment_new)
    average_new = AVERAGE_DECAY * average + (1.0 - AVERAGE_DECAY) * weight_new
    return (weight_new, moment_new, average_new)


def on_device(
    tokens,
    positions,
    counts,
    cotangent,
    qkv_weight,
    out_weight,
    up_weight,
    down_weight,
    small_params,
    qkv_momentum,
    out_momentum,
    up_momentum,
    down_momentum,
    small_momentum,
    qkv_average,
    out_average,
    up_average,
    down_average,
    small_average,
):
    clip_count, seq_len, width = tokens.shape
    row_count = clip_count * seq_len
    head_count = width // HEAD_DIM
    score_scale = HEAD_DIM ** (-0.5)
    low_qkv = qkv_weight.astype(jnp.bfloat16)
    low_out = out_weight.astype(jnp.bfloat16)
    low_up = up_weight.astype(jnp.bfloat16)
    low_down = down_weight.astype(jnp.bfloat16)
    low_small = small_params.astype(jnp.bfloat16)
    wq_full, wo_full, up_full, down_full, small_full = (
        lax.all_gather(low_qkv, "fsdp", axis=0, tiled=True),
        lax.all_gather(low_out, "fsdp", axis=0, tiled=True),
        lax.all_gather(low_up, "fsdp", axis=0, tiled=True),
        lax.all_gather(low_down, "fsdp", axis=0, tiled=True),
        lax.all_gather(low_small, "fsdp", axis=0, tiled=True),
    )
    pieces, bias_up = split_small(small_full)
    gain_one, shift_one, gain_two, shift_two, bias_query, bias_value, bias_out, bias_down = pieces
    key_ok = jnp.arange(seq_len)[None, :] < counts[:, None]
    row_ok = key_ok.reshape(row_count, 1).astype(jnp.float32)
    embed = (tokens.astype(jnp.float32) + sinusoid(positions, width)).reshape(row_count, width)
    hat_one, inv_one = normalize(embed)
    attn_in = (hat_one * gain_one + shift_one).astype(jnp.bfloat16)
    bias_qkv = jnp.concatenate([bias_query, jnp.zeros((width,), jnp.float32), bias_value])
    qkv_rows = (jnp.dot(attn_in, wq_full, preferred_element_type=jnp.float32) + bias_qkv).astype(
        jnp.bfloat16
    )
    query = qkv_rows[:, :width].reshape(clip_count, seq_len, head_count, HEAD_DIM)
    keys = qkv_rows[:, width : 2 * width].reshape(clip_count, seq_len, head_count, HEAD_DIM)
    values = qkv_rows[:, 2 * width :].reshape(clip_count, seq_len, head_count, HEAD_DIM)

    def attention_scores():
        raw = (
            jnp.einsum("clhe,cmhe->chlm", query, keys, preferred_element_type=jnp.float32)
            * score_scale
        )
        return jnp.where(key_ok[:, None, None, :], raw, -1000000000.0)

    scores = attention_scores()
    row_top = jnp.max(scores, axis=-1, keepdims=True)
    expo = jnp.exp(scores - row_top)
    denominator = jnp.sum(expo, axis=-1, keepdims=True)
    log_total = row_top + jnp.log(denominator)
    attention = expo / denominator
    mixed = jnp.einsum(
        "chlm,cmhe->clhe",
        attention.astype(jnp.bfloat16),
        values,
        preferred_element_type=jnp.float32,
    )
    attn_out = mixed.astype(jnp.bfloat16).reshape(row_count, width)
    resid = embed + jnp.dot(attn_out, wo_full, preferred_element_type=jnp.float32) + bias_out
    hat_two, inv_two = normalize(resid)
    mlp_in = (hat_two * gain_two + shift_two).astype(jnp.bfloat16)
    pre = jnp.dot(mlp_in, up_full, preferred_element_type=jnp.float32) + bias_up
    act = jax.nn.gelu(pre, approximate=False).astype(jnp.bfloat16)
    block_rows = resid + jnp.dot(act, down_full, preferred_element_type=jnp.float32) + bias_down
    block_out = block_rows.astype(jnp.bfloat16).reshape(clip_count, seq_len, width)
    wq_full, wo_full, up_full, down_full, small_full = (
        lax.all_gather(low_qkv, "fsdp", axis=0, tiled=True),
        lax.all_gather(low_out, "fsdp", axis=0, tiled=True),
        lax.all_gather(low_up, "fsdp", axis=0, tiled=True),
        lax.all_gather(low_down, "fsdp", axis=0, tiled=True),
        lax.all_gather(low_small, "fsdp", axis=0, tiled=True),
    )
    pieces, bias_up = split_small(small_full)
    gain_one, shift_one, gain_two, shift_two, bias_query, bias_value, bias_out, bias_down = pieces
    grad_rows = cotangent.astype(jnp.float32).reshape(row_count, width) * row_ok
    grad_down = grad_rows.astype(jnp.bfloat16)
    d_bias_down = jnp.sum(grad_down, axis=0, dtype=jnp.float32)
    d_down_weight = jnp.einsum("rf,rd->fd", act, grad_down, preferred_element_type=jnp.float32)
    d_act = jnp.einsum("rd,fd->rf", grad_down, down_full, preferred_element_type=jnp.float32)
    normal_cdf = 0.5 * (1.0 + lax.erf(pre * 0.7071067811865476))
    normal_pdf = jnp.exp(-0.5 * pre * pre) * 0.3989422804014327
    d_pre = (d_act * (normal_cdf + pre * normal_pdf)).astype(jnp.bfloat16)
    d_bias_up = jnp.sum(d_pre, axis=0, dtype=jnp.float32)
    d_up_weight = jnp.einsum("rd,rf->df", mlp_in, d_pre, preferred_element_type=jnp.float32)
    d_mlp_in = jnp.einsum("rf,df->rd", d_pre, up_full, preferred_element_type=jnp.float32)
    d_gain_two = jnp.sum(d_mlp_in * hat_two, axis=0)
    d_shift_two = jnp.sum(d_mlp_in, axis=0)
    d_resid = grad_rows + norm_back(d_mlp_in * gain_two, hat_two, inv_two)
    grad_proj = d_resid.astype(jnp.bfloat16)
    d_bias_out = jnp.sum(grad_proj, axis=0, dtype=jnp.float32)
    d_out_weight = jnp.einsum("rd,re->de", attn_out, grad_proj, preferred_element_type=jnp.float32)
    d_mixed = jnp.einsum("re,de->rd", grad_proj, wo_full, preferred_element_type=jnp.float32)
    d_mixed = d_mixed.astype(jnp.bfloat16).reshape(clip_count, seq_len, head_count, HEAD_DIM)
    attention = jnp.exp(attention_scores() - log_total)
    d_values = jnp.einsum(
        "chlm,clhe->cmhe",
        attention.astype(jnp.bfloat16),
        d_mixed,
        preferred_element_type=jnp.float32,
    )
    d_attention = jnp.einsum("clhe,cmhe->chlm", d_mixed, values, preferred_element_type=jnp.float32)
    inner = jnp.sum(d_attention * attention, axis=-1, keepdims=True)
    d_scores = (attention * (d_attention - inner)).astype(jnp.bfloat16)
    d_query = (
        jnp.einsum("chlm,cmhe->clhe", d_scores, keys, preferred_element_type=jnp.float32)
        * score_scale
    )
    d_keys = (
        jnp.einsum("chlm,clhe->cmhe", d_scores, query, preferred_element_type=jnp.float32)
        * score_scale
    )
    d_qkv = jnp.concatenate(
        [
            d_query.reshape(row_count, width),
            d_keys.reshape(row_count, width),
            d_values.reshape(row_count, width),
        ],
        axis=1,
    ).astype(jnp.bfloat16)
    d_bias_query = jnp.sum(d_qkv[:, :width], axis=0, dtype=jnp.float32)
    d_bias_value = jnp.sum(d_qkv[:, 2 * width :], axis=0, dtype=jnp.float32)
    d_qkv_weight = jnp.einsum("rd,re->de", attn_in, d_qkv, preferred_element_type=jnp.float32)
    d_attn_in = jnp.einsum("re,de->rd", d_qkv, wq_full, preferred_element_type=jnp.float32)
    d_gain_one = jnp.sum(d_attn_in * hat_one, axis=0)
    d_shift_one = jnp.sum(d_attn_in, axis=0)
    token_grad = (d_resid + norm_back(d_attn_in * gain_one, hat_one, inv_one)).reshape(
        clip_count, seq_len, width
    )
    d_columns = jnp.stack(
        [
            d_gain_one,
            d_shift_one,
            d_gain_two,
            d_shift_two,
            d_bias_query,
            d_bias_value,
            d_bias_out,
            d_bias_down,
        ],
        axis=1,
    )
    d_small = jnp.concatenate([d_columns, d_bias_up.reshape(width, -1)], axis=1)
    shard_qkv, shard_out, shard_up, shard_down, shard_small = (
        lax.psum_scatter(d_qkv_weight, "fsdp", scatter_dimension=0, tiled=True),
        lax.psum_scatter(d_out_weight, "fsdp", scatter_dimension=0, tiled=True),
        lax.psum_scatter(d_up_weight, "fsdp", scatter_dimension=0, tiled=True),
        lax.psum_scatter(d_down_weight, "fsdp", scatter_dimension=0, tiled=True),
        lax.psum_scatter(d_small, "fsdp", scatter_dimension=0, tiled=True),
    )
    grads = (
        lax.psum(shard_qkv.astype(jnp.bfloat16), "dp").astype(jnp.float32),
        lax.psum(shard_out.astype(jnp.bfloat16), "dp").astype(jnp.float32),
        lax.psum(shard_up.astype(jnp.bfloat16), "dp").astype(jnp.float32),
        lax.psum(shard_down.astype(jnp.bfloat16), "dp").astype(jnp.float32),
        lax.psum(shard_small.astype(jnp.bfloat16), "dp").astype(jnp.float32),
    )
    masters = (qkv_weight, out_weight, up_weight, down_weight, small_params)
    moments = (qkv_momentum, out_momentum, up_momentum, down_momentum, small_momentum)
    averages = (qkv_average, out_average, up_average, down_average, small_average)
    squares = jnp.stack(
        [jnp.sum(grad * grad) for grad in grads] + [jnp.sum(weight * weight) for weight in masters]
    )
    totals = lax.psum(squares, "fsdp")
    norms = jnp.sqrt(totals)
    results = [
        update_group(masters[i], grads[i], moments[i], averages[i], norms[i], norms[5 + i])
        for i in range(5)
    ]
    return (
        block_out,
        token_grad,
        results[0][0],
        results[1][0],
        results[2][0],
        results[3][0],
        results[4][0],
        results[0][1],
        results[1][1],
        results[2][1],
        results[3][1],
        results[4][1],
        results[0][2],
        results[1][2],
        results[2][2],
        results[3][2],
        results[4][2],
        norms,
    )


def solution(mesh):
    in_specs = (
        P(("dp", "fsdp"), None, None),
        P(("dp", "fsdp"), None),
        P(("dp", "fsdp")),
        P(("dp", "fsdp"), None, None),
        P("fsdp", None),
        P("fsdp", None),
        P("fsdp", None),
        P("fsdp", None),
        P("fsdp", None),
        P("fsdp", None),
        P("fsdp", None),
        P("fsdp", None),
        P("fsdp", None),
        P("fsdp", None),
        P("fsdp", None),
        P("fsdp", None),
        P("fsdp", None),
        P("fsdp", None),
        P("fsdp", None),
    )
    out_specs = (
        P(("dp", "fsdp"), None, None),
        P(("dp", "fsdp"), None, None),
        P("fsdp", None),
        P("fsdp", None),
        P("fsdp", None),
        P("fsdp", None),
        P("fsdp", None),
        P("fsdp", None),
        P("fsdp", None),
        P("fsdp", None),
        P("fsdp", None),
        P("fsdp", None),
        P("fsdp", None),
        P("fsdp", None),
        P("fsdp", None),
        P("fsdp", None),
        P("fsdp", None),
        P(),
    )
    return jax.shard_map(
        on_device, mesh=mesh, in_specs=in_specs, out_specs=out_specs, check_vma=False
    )
```

profile of v0, /device:TPU:0, one launch (start us, length us, event | category | flops | bytes accessed | tf_op | source)
XLA Modules:
  0.0 1200.0 jit_solution(15293713448543002065)
XLA Ops:
  18.3 42.9 %all-gather = bf16[16,48,12]{1,2,0:T(8,128)(2,1)S(1)} all-gather(bf16[1,48,12]{1,2,0:T(8,128)(2,1)S(1)} %get-tuple-element.105), channel_id=1, replica_groups=mesh['dp'=2,'fsdp'=16] {'fsdp'}, dimensions={0}, use_global_device_ids=true | all-gather | bytes 19584 | tf_op jit(solution)/shard_map/all_gather | solution.py:85
  88.2 5.7 add_convert_fusion
  109.2 5.0 reshape.313
  114.2 4.8 copy.178
  119.0 9.3 fusion.22
  128.3 11.1 fusion
  139.4 9.1 fusion.32
  156.8 69.6 %all-gather.10.cloned.1.call-done = bf16[768,3072]{1,0:T(8,128)(2,1)} async-done(((bf16[48,3072]{1,0:T(8,128)(2,1)}), bf16[768,3072]{1,0:T(8,128)(2,1)}) %all-gather.10.cloned.1.call-update) | async-done | bytes 4718608 | tf_op jit(solution)/shard_map/all_gather | solution.py:83
  226.4 27.8 %fusion.4 = (bf16[784,3072]{1,0:T(8,128)(2,1)}, f32[784,3072]{1,0:T(8,128)}) fusion(f32[3072]{0:T(1024)S(1)} %reshape.306, bf16[768,3072]{1,0:T(8,128)(2,1)} %all-gather.10.cloned.1.call-done, f32[768]{0:T(1024)S(1)} %get-tuple-element.63, f32[768]{0:T(1024)S(1)} %get-tuple-element.64, f32[784]{0:T(1024)S(1)} %add_rsqrt_fusion, ...), kind=kOutput, calls=%fused_computation.12 | convolution fusion | flops 3861946368 | bytes 21605504 | tf_op jit(solution)/shard_map/dot_general | solution.py:125
  254.3 54.5 %all-gather.12.cloned.1.call-done = bf16[3072,768]{1,0:T(8,128)(2,1)} async-done(((bf16[192,768]{1,0:T(8,128)(2,1)}), bf16[3072,768]{1,0:T(8,128)(2,1)}) %all-gather.12.cloned.1.call-update) | async-done | bytes 4718608 | tf_op jit(solution)/shard_map/all_gather | solution.py:84
  308.8 10.0 convert_reduce_fusion
  333.6 4.8 reshape.316
  338.4 4.9 copy.183
  343.2 15.5 %multiply_reduce_fusion = (f32[2,12,392]{2,1,0:T(8,128)S(1)}, f32[2,12,392,392]{2,3,1,0:T(8,128)}) fusion(f32[2,12,392]{2,1,0:T(8,128)S(1)} %log_add_fusion, f32[2,12,392,392]{2,3,1,0:T(8,128)} %get-tuple-element.121, pred[2,392]{1,0:T(4,128)(4,1)S(1)} %get-tuple-element.119, bf16[2,392,12,64]{1,3,2,0:T(8,128)(2,1)} %copy.183, ...), kind=kOutput, calls=%fused_computation.1 | convolution fusion | flops 490486080 | bytes 31987984 | tf_op jit(solution)/shard_map/clhe,cmhe->chlm/dot_general | solution.py:164
  358.7 9.1 fusion.29
  370.6 4.7 reshape.296
  375.3 14.8 %multiply_convert_fusion = bf16[2,12,392,392]{2,3,1,0:T(8,128)(2,1)S(1)} fusion(f32[2,12,392,392]{2,3,1,0:T(8,128)} %get-tuple-element.124, f32[2,12,392]{2,1,0:T(8,128)S(1)} %get-tuple-element.123, f32[2,12,392]{2,1,0:T(8,128)S(1)} %log_add_fusion, f32[2,12,392,392]{2,3,1,0:T(8,128)} %get-tuple-element.121, pred[2,392]{1,0:T(4,128)(4,1)S(1)} %get-tuple-element.119), kind=kLoop, calls=%fused_computation | loop fusion | flops 22127616 | bytes 36955408 | tf_op jit(solution)/shard_map/convert_element_type | solution.py:166
  396.6 4.8 reshape.294
  401.3 7.2 fusion.34
  411.3 5.0 reshape.295
  420.7 6.0 fusion.38
  426.8 10.3 fusion.39
  437.1 9.5 fusion.62
  452.8 8.9 multiply_reduce_fusion.3
  464.4 148.5 %reduce-scatter.8.cloned.1.call-done = f32[48,2304]{1,0:T(8,128)} async-done(((f32[768,2304]{1,0:T(8,128)}), f32[48,2304]{1,0:T(8,128)}) %reduce-scatter.8.cloned.1.call-update) | async-done | bytes 442384 | tf_op jit(solution)/shard_map/reduce_scatter | solution.py:207
  614.6 174.0 %reduce-scatter.12.cloned.1.call-done = f32[48,3072]{1,0:T(8,128)} async-done(((f32[768,3072]{1,0:T(8,128)}), f32[48,3072]{1,0:T(8,128)}) %reduce-scatter.12.cloned.1.call-update) | async-done | bytes 589840 | tf_op jit(solution)/shard_map/reduce_scatter | solution.py:209
  790.4 173.9 %reduce-scatter.14.cloned.1.call-done = f32[192,768]{1,0:T(8,128)} async-done(((f32[3072,768]{1,0:T(8,128)}), f32[192,768]{1,0:T(8,128)}) %reduce-scatter.14.cloned.1.call-update) | async-done | bytes 589840 | tf_op jit(solution)/shard_map/reduce_scatter | solution.py:210
  966.2 8.7 add_convert_fusion.1
  974.9 115.7 %reduce-scatter.16.cloned.1.call-done = f32[48,12]{1,0:T(8,128)} async-done(((f32[768,12]{1,0:T(8,128)}), f32[48,12]{1,0:T(8,128)}) %reduce-scatter.16.cloned.1.call-update) | async-done | bytes 2320
  1094.5 18.2 %all-reduce.3.cloned.1.call-done = (bf16[48,2304]{1,0:T(8,128)(2,1)}, bf16[48,768]{1,0:T(8,128)(2,1)}, bf16[48,3072]{1,0:T(8,128)(2,1)}, bf16[192,768]{1,0:T(8,128)(2,1)}) async-done(((bf16[48,2304]{1,0:T(8,128)(2,1)}, bf16[48,768]{1,0:T(8,128)(2,1)}, bf16[48,3072]{1,0:T(8,128)(2,1)}, bf16[192,768]{1,0:T(8,128)(2,1)}), (bf16[48,2304]{1,0:T(8,128)(2,1)}, bf16[48,768]{1,0:T(8,128)(2,1)}, ...) | async-done | bytes 884752 | tf_op jit(solution)/shard_map/psum | solution.py:214
  1119.3 6.5 stack.81
  1130.6 42.6 %psum.47 = f32[10]{0:T(128)} all-reduce(f32[10]{0:T(128)S(1)} %stack.81), channel_id=1, replica_groups=mesh['dp'=2,'fsdp'=16] {'fsdp'}, use_global_device_ids=true, to_apply=%region_40.41 | all-reduce | flops 10 | bytes 80 | tf_op jit(solution)/shard_map/psum | solution.py:226
  (212 shorter events, 131.3 us)
Async XLA Ops:
  7.2 54.8 %copy-start.46 = (s32[2,392]{1,0:T(2,128)S(1)}, s32[2,392]{1,0:T(2,128)}, u32[]{:S(2)}) copy-start(s32[2,392]{1,0:T(2,128)} %param.20) | copy-start | bytes 9412
  7.2 54.8 %copy-start.17 = (bf16[2,392,768]{2,1,0:T(8,128)(2,1)S(1)}, bf16[2,392,768]{2,1,0:T(8,128)(2,1)}, u32[]{:S(2)}) copy-start(bf16[2,392,768]{2,1,0:T(8,128)(2,1)} %param.19) | copy-start | bytes 3612676
  7.2 81.0 %all-gather.6.cloned.1.call-start = ((), (), s32[]{:S(2)}) async-start(), calls=%async_computation.5 | async-start | bytes 3760128 | tf_op jit(solution)/shard_map/all_gather | solution.py:81
  9.8 142.4 %all-gather.8.cloned.1.call-start = ((), (), s32[]{:S(2)}) async-start(), calls=%async_computation.6 | async-start | bytes 1253376 | tf_op jit(solution)/shard_map/all_gather | solution.py:82
  12.2 214.3 %all-gather.10.cloned.1.call-start = ((), (), s32[]{:S(2)}) async-start(), calls=%async_computation.7 | async-start | bytes 5013504 | tf_op jit(solution)/shard_map/all_gather | solution.py:83
  14.9 293.9 %all-gather.12.cloned.1.call-start = ((), (), s32[]{:S(2)}) async-start(), calls=%async_computation.8 | async-start | bytes 5013504 | tf_op jit(solution)/shard_map/all_gather | solution.py:84
  17.7 445.1 %reduce-scatter.10.cloned.1.call-start = ((), (), s32[]{:S(2)}) async-start(), calls=%async_computation.10 | async-start | bytes 2506752 | tf_op jit(solution)/shard_map/reduce_scatter | solution.py:208
  62.0 26.2 %copy-start.41 = (f32[768]{0:T(1024)}, f32[768]{0:T(1024)S(1)}, u32[]{:S(2)}) copy-start(f32[768]{0:T(1024)S(1)} %get-tuple-element.69) | copy-start | bytes 9220
  62.0 26.2 %copy-start.44 = (f32[768]{0:T(1024)}, f32[768]{0:T(1024)S(1)}, u32[]{:S(2)}) copy-start(f32[768]{0:T(1024)S(1)} %get-tuple-element.68) | copy-start | bytes 9220
  102.1 16.8 %copy-start.2 = (bf16[2,392,12,64]{1,3,2,0:T(8,128)(2,1)}, bf16[2,392,12,64]{1,3,2,0:T(8,128)(2,1)S(1)}, u32[]{:S(2)}) copy-start(bf16[2,392,12,64]{1,3,2,0:T(8,128)(2,1)S(1)} %copy.177) | copy-start | bytes 3612676
  329.4 283.5 %reduce-scatter.8.cloned.1.call-start = ((), (), s32[]{:S(2)}) async-start(), calls=%async_computation.9 | async-start | bytes 7520256 | tf_op jit(solution)/shard_map/reduce_scatter | solution.py:207
  343.2 15.5 %copy-start.9 = (bf16[2,392,12,64]{1,3,2,0:T(8,128)(2,1)S(1)}, bf16[2,392,12,64]{1,3,2,0:T(8,128)(2,1)}, u32[]{:S(2)}) copy-start(bf16[2,392,12,64]{1,3,2,0:T(8,128)(2,1)} %copy.183) | copy-start | bytes 3612676
  375.3 14.8 %copy-start.3 = (bf16[2,392,12,64]{1,3,2,0:T(8,128)(2,1)S(1)}, bf16[2,392,12,64]{1,3,2,0:T(8,128)(2,1)}, u32[]{:S(2)}) copy-start(bf16[2,392,12,64]{1,3,2,0:T(8,128)(2,1)} %copy-done.2) | copy-start | bytes 3612676
  426.7 361.9 %reduce-scatter.12.cloned.1.call-start = ((), (), s32[]{:S(2)}) async-start(), calls=%async_computation.11 | async-start | bytes 10027008 | tf_op jit(solution)/shard_map/reduce_scatter | solution.py:209
  437.1 527.2 %reduce-scatter.14.cloned.1.call-start = ((), (), s32[]{:S(2)}) async-start(), calls=%async_computation.12 | async-start | bytes 10027008 | tf_op jit(solution)/shard_map/reduce_scatter | solution.py:210
  446.6 643.9 %reduce-scatter.16.cloned.1.call-start = ((), (), s32[]{:S(2)}) async-start(), calls=%async_computation.13 | async-start | bytes 417792
  461.7 504.4 %copy-start.43 = (f32[768]{0:T(1024)S(1)}, f32[768]{0:T(1024)}, u32[]{:S(2)}) copy-start(f32[768]{0:T(1024)} %get-tuple-element.62) | copy-start | bytes 9220
  462.7 649.9 %all-reduce.3.cloned.1.call-start = ((), (), s32[]{:S(2)}) async-start(), calls=%async_computation.14 | async-start | bytes 1769472 | tf_op jit(solution)/shard_map/psum | solution.py:214
  966.1 159.7 %copy-start.34 = (f32[784]{0:T(1024)S(1)}, f32[784]{0:T(1024)}, u32[]{:S(2)}) copy-start(f32[784]{0:T(1024)} %copy-done.33) | copy-start | bytes 9412
  966.1 159.7 %copy-start.36 = (f32[784]{0:T(1024)S(1)}, f32[784]{0:T(1024)}, u32[]{:S(2)}) copy-start(f32[784]{0:T(1024)} %copy-done.35) | copy-start | bytes 9412
  1125.8 58.6 %copy-start.40 = (f32[48,12]{0,1:T(8,128)S(1)}, f32[48,12]{0,1:T(8,128)}, u32[]{:S(2)}) copy-start(f32[48,12]{0,1:T(8,128)} %param.27) | copy-start | bytes 6916
  1125.8 59.9 %copy-start.21 = (f32[48,768]{1,0:T(8,128)S(1)}, f32[48,768]{1,0:T(8,128)}, u32[]{:S(2)}) copy-start(f32[48,768]{1,0:T(8,128)} %param.24) | copy-start | bytes 442372
  1125.8 59.9 %copy-start.28 = (bf16[48,768]{1,0:T(8,128)(2,1)S(1)}, bf16[48,768]{1,0:T(8,128)(2,1)}, u32[]{:S(2)}) copy-start(bf16[48,768]{1,0:T(8,128)(2,1)} %get-tuple-element.71) | copy-start | bytes 221188
  1125.9 59.9 %copy-start.29 = (f32[48,768]{1,0:T(8,128)S(1)}, f32[48,768]{1,0:T(8,128)}, u32[]{:S(2)}) copy-start(f32[48,768]{1,0:T(8,128)} %param.34) | copy-start | bytes 442372
  1125.9 61.6 %copy-start.15 = (f32[48,2304]{1,0:T(8,128)S(1)}, f32[48,2304]{1,0:T(8,128)}, u32[]{:S(2)}) copy-start(f32[48,2304]{1,0:T(8,128)} %param.23) | copy-start | bytes 1327108
  1125.9 61.6 %copy-start.20 = (bf16[48,2304]{1,0:T(8,128)(2,1)S(1)}, bf16[48,2304]{1,0:T(8,128)(2,1)}, u32[]{:S(2)}) copy-start(bf16[48,2304]{1,0:T(8,128)(2,1)} %get-tuple-element.70) | copy-start | bytes 663556
  1125.9 61.6 %copy-start.27 = (f32[48,2304]{1,0:T(8,128)S(1)}, f32[48,2304]{1,0:T(8,128)}, u32[]{:S(2)}) copy-start(f32[48,2304]{1,0:T(8,128)} %param.33) | copy-start | bytes 1327108
  1130.5 59.3 %copy-start.13 = (f32[192,768]{1,0:T(8,128)S(1)}, f32[192,768]{1,0:T(8,128)}, u32[]{:S(2)}) copy-start(f32[192,768]{1,0:T(8,128)} %param.26) | copy-start | bytes 1769476
  1130.5 59.3 %copy-start.19 = (bf16[192,768]{1,0:T(8,128)(2,1)S(1)}, bf16[192,768]{1,0:T(8,128)(2,1)}, u32[]{:S(2)}) copy-start(bf16[192,768]{1,0:T(8,128)(2,1)} %get-tuple-element.73) | copy-start | bytes 884740
  1130.5 59.3 %copy-start.22 = (f32[192,768]{1,0:T(8,128)S(1)}, f32[192,768]{1,0:T(8,128)}, u32[]{:S(2)}) copy-start(f32[192,768]{1,0:T(8,128)} %param.36) | copy-start | bytes 1769476
  1130.6 59.3 %copy-start.23 = (f32[192,768]{1,0:T(8,128)S(1)}, f32[192,768]{1,0:T(8,128)}, u32[]{:S(2)}) copy-start(f32[192,768]{1,0:T(8,128)} %param.31) | copy-start | bytes 1769476
  1173.9 17.4 %copy-start.30 = (f32[10]{0:T(128)}, f32[10]{0:T(128)S(1)}, u32[]{:S(2)}) copy-start(f32[10]{0:T(128)S(1)} %sqrt.3) | copy-start | bytes 124
  (27 other events, 118.8 us)
Sparse Core Ops, SparseCore 0:
  11.4 74.0 all-gather.5
  88.9 54.6 all-gather.7
  147.0 79.3 all-gather.9
  229.6 79.0 all-gather.11
  329.5 126.9 reduce-scatter.9
  462.5 150.3 reduce-scatter.7
  619.5 169.0 reduce-scatter.11
  794.3 169.9 reduce-scatter.13
  970.2 120.3 reduce-scatter.15
  1094.1 18.4 all-reduce.2
where the time goes:
time: 1210 us; the launch traced here: 1200 us
  waiting for transfers between devices  755 us (62%)
  matrix products  154 us (13%)
  local copies, waits for them, and re-layouts  90.5 us (7%)
  blocking collectives  88 us (7%)
  other arithmetic  86.6 us (7%)
  between operations  25.3 us (2%)
    reduce_scatter x1, waiting for transfers between devices, on_device(): lax.psum_scatter(d_up_weight, 'fsdp', scatter_dimension=0, tiled=True)  174 us
    reduce_scatter x1, waiting for transfers between devices, on_device(): lax.psum_scatter(d_down_weight, 'fsdp', scatter_dimension=0, tiled=True)  174 us
    reduce_scatter x1, waiting for transfers between devices, on_device(): lax.psum_scatter(d_qkv_weight, 'fsdp', scatter_dimension=0, tiled=True)  149 us
    unnamed x11, waiting for transfers between devices  116 us
    all_gather x1, waiting for transfers between devices, on_device(): lax.all_gather(low_up, 'fsdp', axis=0, tiled=True)  69.6 us
    all_gather x1, waiting for transfers between devices, on_device(): lax.all_gather(low_down, 'fsdp', axis=0, tiled=True)  54.5 us
    all_gather x1, blocking collectives, on_device(): lax.all_gather(low_small, 'fsdp', axis=0, tiled=True)  42.9 us
    psum x1, blocking collectives, on_device(): totals = lax.psum(squares, 'fsdp')  42.6 us
  transfers between devices with their start and end apart: 10, of which 7 were waited for; matrix products, arithmetic and copies ran while one was open for 23% of the time, Pallas kernels for 0%

commit v1 on v0

--- a/solution.py
+++ b/solution.py
@@ -10,6 +10,19 @@
 WEIGHT_DECAY = 0.0001
 TRUST_RATE = 0.2
 AVERAGE_DECAY = 0.8
+
+
+def collect(x, axis, dim):
+    size, position, rows = (lax.axis_size(axis), lax.axis_index(axis), x.shape[dim])
+    right = [(i, (i + 1) % size) for i in range(size)]
+    whole = jnp.zeros((*x.shape[:dim], size * rows, *x.shape[dim + 1 :]), x.dtype)
+    held = x
+    for lap in range(size):
+        owner = (position - lap) % size
+        whole = lax.dynamic_update_slice_in_dim(whole, held, owner * rows, axis=dim)
+        if lap < size - 1:
+            held = lax.ppermute(held, axis, right)
+    return whole
 
 
 def sinusoid(positions, width):
@@ -81,7 +94,7 @@
         lax.all_gather(low_qkv, "fsdp", axis=0, tiled=True),
         lax.all_gather(low_out, "fsdp", axis=0, tiled=True),
         lax.all_gather(low_up, "fsdp", axis=0, tiled=True),
-        lax.all_gather(low_down, "fsdp", axis=0, tiled=True),
+        collect(low_down, "fsdp", 0),
         lax.all_gather(low_small, "fsdp", axis=0, tiled=True),
     )
     pieces, bias_up = split_small(small_full)

time: 1210 us -> 1260 us (1.041)
  local copies, waits for them, and re-layouts: 90.5 us -> 116 us
  waiting for transfers between devices: 755 us -> 779 us
    ppermute x0 -> x15, waiting for transfers between devices: none -> 180 us  [collect(): held = lax.ppermute(held, axis, right)]
    reduce_scatter x1, waiting for transfers between devices: 149 us -> 0.01 us  [on_device(): lax.psum_scatter(d_qkv_weight, 'fsdp', scatter_dimension=0, tiled=True)]
    dynamic_update_slice x0 -> x15, local copies, waits for them, and re-layouts: none -> 18.9 us  [collect(): whole = lax.dynamic_update_slice_in_dim(whole, held, owner * rows, axis=dim)]
  transfers between devices with their start and end apart: 10 -> 25, of which waited for: 7 -> 21; matrix products, arithmetic and copies ran while one was open for 23% -> 24% of each run, Pallas kernels for 0% -> 0%
where the time goes in v1:
time: 1260 us; the launch traced here: 1250 us
  waiting for transfers between devices  779 us (62%)
  matrix products  154 us (12%)
  local copies, waits for them, and re-layouts  116 us (9%)
  blocking collectives  87.6 us (7%)
  other arithmetic  83.7 us (7%)
  between operations  25.4 us (2%)
    ppermute x15, waiting for transfers between devices, collect(): held = lax.ppermute(held, axis, right)  180 us
    reduce_scatter x1, waiting for transfers between devices, on_device(): lax.psum_scatter(d_down_weight, 'fsdp', scatter_dimension=0, tiled=True)  174 us
    reduce_scatter x1, waiting for transfers between devices, on_device(): lax.psum_scatter(d_up_weight, 'fsdp', scatter_dimension=0, tiled=True)  167 us
    unnamed x11, waiting for transfers between devices  116 us
    all_gather x1, waiting for transfers between devices, on_device(): lax.all_gather(low_up, 'fsdp', axis=0, tiled=True)  69.2 us
    all_gather x1, waiting for transfers between devices, on_device(): lax.all_gather(low_down, 'fsdp', axis=0, tiled=True)  54.5 us
    all_gather x1, blocking collectives, on_device(): lax.all_gather(low_small, 'fsdp', axis=0, tiled=True)  43 us
    psum x1, blocking collectives, on_device(): totals = lax.psum(squares, 'fsdp')  42.1 us
  transfers between devices with their start and end apart: 25, of which 21 were waited for; matrix products, arithmetic and copies ran while one was open for 24% of the time, Pallas kernels for 0%

profile of v1, /device:TPU:0, one launch (start us, length us, event | category | flops | bytes accessed | tf_op | source)
XLA Modules:
  0.0 1248.2 jit_solution(12702171634024828418)
XLA Ops:
  18.9 43.0 %all-gather = bf16[16,48,12]{1,2,0:T(8,128)(2,1)S(1)} all-gather(bf16[1,48,12]{1,2,0:T(8,128)(2,1)S(1)} %get-tuple-element.105), channel_id=1, replica_groups=mesh['dp'=2,'fsdp'=16] {'fsdp'}, dimensions={0}, use_global_device_ids=true | all-gather | bytes 19584 | tf_op jit(solution)/shard_map/all_gather | solution.py:98
  119.5 9.3 fusion.22
  128.9 10.9 fusion
  139.8 9.1 fusion.32
  157.3 69.2 %all-gather.10.cloned.1.call-done = bf16[768,3072]{1,0:T(8,128)(2,1)} async-done(((bf16[48,3072]{1,0:T(8,128)(2,1)}), bf16[768,3072]{1,0:T(8,128)(2,1)}) %all-gather.10.cloned.1.call-update) | async-done | bytes 4718608 | tf_op jit(solution)/shard_map/all_gather | solution.py:96
  226.4 27.8 %fusion.4 = (bf16[784,3072]{1,0:T(8,128)(2,1)}, f32[784,3072]{1,0:T(8,128)}) fusion(f32[3072]{0:T(1024)S(1)} %reshape.306, bf16[768,3072]{1,0:T(8,128)(2,1)} %all-gather.10.cloned.1.call-done, f32[768]{0:T(1024)S(1)} %get-tuple-element.63, f32[768]{0:T(1024)S(1)} %get-tuple-element.64, f32[784]{0:T(1024)S(1)} %add_rsqrt_fusion, ...), kind=kOutput, calls=%fused_computation.12 | convolution fusion | flops 3861946368 | bytes 21605504 | tf_op jit(solution)/shard_map/dot_general | solution.py:138
  254.3 54.5 %all-gather.12.cloned.1.call-done = bf16[3072,768]{1,0:T(8,128)(2,1)} async-done(((bf16[192,768]{1,0:T(8,128)(2,1)}), bf16[3072,768]{1,0:T(8,128)(2,1)}) %all-gather.12.cloned.1.call-update) | async-done | bytes 4718608 | tf_op jit(solution)/shard_map/all_gather | solution.py:146
  308.8 10.0 convert_reduce_fusion
  343.3 15.5 %multiply_reduce_fusion = (f32[2,12,392]{2,1,0:T(8,128)S(1)}, f32[2,12,392,392]{2,3,1,0:T(8,128)}) fusion(f32[2,12,392]{2,1,0:T(8,128)S(1)} %log_add_fusion, f32[2,12,392,392]{2,3,1,0:T(8,128)} %get-tuple-element.121, pred[2,392]{1,0:T(4,128)(4,1)S(1)} %get-tuple-element.119, bf16[2,392,12,64]{1,3,2,0:T(8,128)(2,1)} %copy.183, ...), kind=kOutput, calls=%fused_computation.1 | convolution fusion | flops 490486080 | bytes 31987984 | tf_op jit(solution)/shard_map/clhe,cmhe->chlm/dot_general | solution.py:177
  358.7 9.1 fusion.29
  375.4 14.8 %multiply_convert_fusion = bf16[2,12,392,392]{2,3,1,0:T(8,128)(2,1)S(1)} fusion(f32[2,12,392,392]{2,3,1,0:T(8,128)} %get-tuple-element.124, f32[2,12,392]{2,1,0:T(8,128)S(1)} %get-tuple-element.123, f32[2,12,392]{2,1,0:T(8,128)S(1)} %log_add_fusion, f32[2,12,392,392]{2,3,1,0:T(8,128)} %get-tuple-element.121, pred[2,392]{1,0:T(4,128)(4,1)S(1)} %get-tuple-element.119), kind=kLoop, calls=%fused_computation | loop fusion | flops 22127616 | bytes 36955408 | tf_op jit(solution)/shard_map/convert_element_type | solution.py:179
  427.9 10.3 fusion.39
  438.2 9.5 fusion.62
  450.1 11.2 collective-permute-done
  462.1 11.1 collective-permute-done.1
  473.2 18.5 %collective-permute-done.2 = bf16[192,768]{1,0:T(8,128)(2,1)S(1)} collective-permute-done((bf16[192,768]{1,0:T(8,128)(2,1)S(1)}, bf16[192,768]{1,0:T(8,128)(2,1)S(1)}, u32[]{:S(2)}, u32[]{:S(2)}) %collective-permute-start.2) | collective-permute-done | bytes 294944 | tf_op jit(solution)/shard_map/ppermute | solution.py:24
  491.7 18.3 %collective-permute-done.3 = bf16[192,768]{1,0:T(8,128)(2,1)S(1)} collective-permute-done((bf16[192,768]{1,0:T(8,128)(2,1)S(1)}, bf16[192,768]{1,0:T(8,128)(2,1)S(1)}, u32[]{:S(2)}, u32[]{:S(2)}) %collective-permute-start.3) | collective-permute-done | bytes 294944 | tf_op jit(solution)/shard_map/ppermute | solution.py:24
  510.8 16.8 %collective-permute-done.4 = bf16[192,768]{1,0:T(8,128)(2,1)S(1)} collective-permute-done((bf16[192,768]{1,0:T(8,128)(2,1)S(1)}, bf16[192,768]{1,0:T(8,128)(2,1)S(1)}, u32[]{:S(2)}, u32[]{:S(2)}) %collective-permute-start.4) | collective-permute-done | bytes 294944 | tf_op jit(solution)/shard_map/ppermute | solution.py:24
  528.3 10.9 collective-permute-done.5
  539.9 10.5 collective-permute-done.6
  550.4 10.5 collective-permute-done.7
  560.9 10.6 collective-permute-done.8
  573.8 10.5 collective-permute-done.9
  588.6 9.3 collective-permute-done.10
  614.9 15.0 %collective-permute-done.12 = bf16[192,768]{1,0:T(8,128)(2,1)S(1)} collective-permute-done((bf16[192,768]{1,0:T(8,128)(2,1)S(1)}, bf16[192,768]{1,0:T(8,128)(2,1)S(1)}, u32[]{:S(2)}, u32[]{:S(2)}) %collective-permute-start.12) | collective-permute-done | bytes 294944 | tf_op jit(solution)/shard_map/ppermute | solution.py:24
  644.7 9.7 collective-permute-done.14
  659.0 8.9 multiply_reduce_fusion.3
  672.4 167.5 %reduce-scatter.12.cloned.1.call-done = f32[48,3072]{1,0:T(8,128)} async-done(((f32[768,3072]{1,0:T(8,128)}), f32[48,3072]{1,0:T(8,128)}) %reduce-scatter.12.cloned.1.call-update) | async-done | bytes 589840 | tf_op jit(solution)/shard_map/reduce_scatter | solution.py:222
  841.7 173.7 %reduce-scatter.14.cloned.1.call-done = f32[192,768]{1,0:T(8,128)} async-done(((f32[3072,768]{1,0:T(8,128)}), f32[192,768]{1,0:T(8,128)}) %reduce-scatter.14.cloned.1.call-update) | async-done | bytes 589840 | tf_op jit(solution)/shard_map/reduce_scatter | solution.py:223
  1025.9 115.7 %reduce-scatter.16.cloned.1.call-done = f32[48,12]{1,0:T(8,128)} async-done(((f32[768,12]{1,0:T(8,128)}), f32[48,12]{1,0:T(8,128)}) %reduce-scatter.16.cloned.1.call-update) | async-done | bytes 2320
  1145.5 18.2 %all-reduce.3.cloned.1.call-done = (bf16[48,2304]{1,0:T(8,128)(2,1)}, bf16[48,768]{1,0:T(8,128)(2,1)}, bf16[48,3072]{1,0:T(8,128)(2,1)}, bf16[192,768]{1,0:T(8,128)(2,1)}) async-done(((bf16[48,2304]{1,0:T(8,128)(2,1)}, bf16[48,768]{1,0:T(8,128)(2,1)}, bf16[48,3072]{1,0:T(8,128)(2,1)}, bf16[192,768]{1,0:T(8,128)(2,1)}), (bf16[48,2304]{1,0:T(8,128)(2,1)}, bf16[48,768]{1,0:T(8,128)(2,1)}, ...) | async-done | bytes 884752 | tf_op jit(solution)/shard_map/psum | solution.py:227
  1181.6 42.1 %psum.47 = f32[10]{0:T(128)S(1)} all-reduce(f32[10]{0:T(128)S(1)} %stack.81), channel_id=1, replica_groups=mesh['dp'=2,'fsdp'=16] {'fsdp'}, use_global_device_ids=true, to_apply=%region_40.41 | all-reduce | flops 10 | bytes 80 | tf_op jit(solution)/shard_map/psum | solution.py:239
  (289 shorter events, 240.6 us)
Async XLA Ops:
  7.2 81.6 %all-gather.6.cloned.1.call-start = ((), (), s32[]{:S(2)}) async-start(), calls=%async_computation.5 | async-start | bytes 3760128 | tf_op jit(solution)/shard_map/all_gather | solution.py:94
  9.8 142.9 %all-gather.8.cloned.1.call-start = ((), (), s32[]{:S(2)}) async-start(), calls=%async_computation.6 | async-start | bytes 1253376 | tf_op jit(solution)/shard_map/all_gather | solution.py:95
  12.2 214.2 %all-gather.10.cloned.1.call-start = ((), (), s32[]{:S(2)}) async-start(), calls=%async_computation.7 | async-start | bytes 5013504 | tf_op jit(solution)/shard_map/all_gather | solution.py:96
  15.0 293.8 %all-gather.12.cloned.1.call-start = ((), (), s32[]{:S(2)}) async-start(), calls=%async_computation.8 | async-start | bytes 5013504 | tf_op jit(solution)/shard_map/all_gather | solution.py:146
  18.3 650.8 %reduce-scatter.10.cloned.1.call-start = ((), (), s32[]{:S(2)}) async-start(), calls=%async_computation.10 | async-start | bytes 2506752 | tf_op jit(solution)/shard_map/reduce_scatter | solution.py:221
  329.4 341.2 %reduce-scatter.8.cloned.1.call-start = ((), (), s32[]{:S(2)}) async-start(), calls=%async_computation.9 | async-start | bytes 7520256 | tf_op jit(solution)/shard_map/reduce_scatter | solution.py:220
  427.8 412.0 %reduce-scatter.12.cloned.1.call-start = ((), (), s32[]{:S(2)}) async-start(), calls=%async_computation.11 | async-start | bytes 10027008 | tf_op jit(solution)/shard_map/reduce_scatter | solution.py:222
  438.2 577.2 %reduce-scatter.14.cloned.1.call-start = ((), (), s32[]{:S(2)}) async-start(), calls=%async_computation.12 | async-start | bytes 10027008 | tf_op jit(solution)/shard_map/reduce_scatter | solution.py:223
  447.7 124.5 %copy-start.51 = (f32[2,392]{1,0:T(2,128)S(1)}, f32[2,392]{1,0:T(2,128)}, u32[]{:S(2)}) copy-start(f32[2,392]{1,0:T(2,128)} %copy-done.50) | copy-start | bytes 9412
  447.7 136.6 %copy-start.11 = (f32[192,768]{1,0:T(8,128)S(1)}, f32[192,768]{1,0:T(8,128)}, u32[]{:S(2)}) copy-start(f32[192,768]{1,0:T(8,128)} %param.26) | copy-start | bytes 1769476
  447.8 693.9 %reduce-scatter.16.cloned.1.call-start = ((), (), s32[]{:S(2)}) async-start(), calls=%async_computation.13 | async-start | bytes 417792
  448.7 12.7 %collective-permute-start = (bf16[192,768]{1,0:T(8,128)(2,1)S(1)}, bf16[192,768]{1,0:T(8,128)(2,1)S(1)}, u32[]{:S(2)}, u32[]{:S(2)}) collective-permute-start(bf16[192,768]{1,0:T(8,128)(2,1)S(1)} %copy-done.21), channel_id=1, source_target_pairs={{0,1},{1,2},{2,3},{3,4},{4,5},{5,6},{6,7},{7,8},{8,9},{9,10},{10,1... | collective-permute-start | bytes 884744 | tf_op jit(solution)/shard_map/ppermute | solution.py:24
  462.1 11.1 collective-permute-start.1
  473.2 77.2 %copy-start.34 = (bf16[192,768]{1,0:T(8,128)(2,1)}, bf16[192,768]{1,0:T(8,128)(2,1)S(1)}, u32[]{:S(2)}) copy-start(bf16[192,768]{1,0:T(8,128)(2,1)S(1)} %collective-permute-done.1) | copy-start | bytes 884740
  473.2 18.5 %collective-permute-start.2 = (bf16[192,768]{1,0:T(8,128)(2,1)S(1)}, bf16[192,768]{1,0:T(8,128)(2,1)S(1)}, u32[]{:S(2)}, u32[]{:S(2)}) collective-permute-start(bf16[192,768]{1,0:T(8,128)(2,1)S(1)} %collective-permute-done.1), channel_id=1, source_target_pairs={{0,1},{1,2},{2,3},{3,4},{4,5},{5,6},{6,7},{7,8},{8,9},{9,10},{10,1... | collective-permute-start | bytes 884744 | tf_op jit(solution)/shard_map/ppermute | solution.py:24
  491.7 18.3 %collective-permute-start.3 = (bf16[192,768]{1,0:T(8,128)(2,1)S(1)}, bf16[192,768]{1,0:T(8,128)(2,1)S(1)}, u32[]{:S(2)}, u32[]{:S(2)}) collective-permute-start(bf16[192,768]{1,0:T(8,128)(2,1)S(1)} %collective-permute-done.2), channel_id=1, source_target_pairs={{0,1},{1,2},{2,3},{3,4},{4,5},{5,6},{6,7},{7,8},{8,9},{9,10},{10,1... | collective-permute-start | bytes 884744 | tf_op jit(solution)/shard_map/ppermute | solution.py:24
  510.1 17.5 %collective-permute-start.4 = (bf16[192,768]{1,0:T(8,128)(2,1)S(1)}, bf16[192,768]{1,0:T(8,128)(2,1)S(1)}, u32[]{:S(2)}, u32[]{:S(2)}) collective-permute-start(bf16[192,768]{1,0:T(8,128)(2,1)S(1)} %collective-permute-done.3), channel_id=1, source_target_pairs={{0,1},{1,2},{2,3},{3,4},{4,5},{5,6},{6,7},{7,8},{8,9},{9,10},{10,1... | collective-permute-start | bytes 884744 | tf_op jit(solution)/shard_map/ppermute | solution.py:24
  527.6 11.6 collective-permute-start.5
  539.9 10.5 collective-permute-start.6
  550.4 10.5 collective-permute-start.7
  560.9 10.6 collective-permute-start.8
  572.2 12.1 collective-permute-start.9
  584.4 13.5 %collective-permute-start.10 = (bf16[192,768]{1,0:T(8,128)(2,1)}, bf16[192,768]{1,0:T(8,128)(2,1)}, u32[]{:S(2)}, u32[]{:S(2)}) collective-permute-start(bf16[192,768]{1,0:T(8,128)(2,1)} %collective-permute-done.9), channel_id=1, source_target_pairs={{0,1},{1,2},{2,3},{3,4},{4,5},{5,6},{6,7},{7,8},{8,9},{9,10},{10,1... | collective-permute-start | bytes 884744 | tf_op jit(solution)/shard_map/ppermute | solution.py:24
  597.8 12.9 %collective-permute-start.11 = (bf16[192,768]{1,0:T(8,128)(2,1)}, bf16[192,768]{1,0:T(8,128)(2,1)S(1)}, u32[]{:S(2)}, u32[]{:S(2)}) collective-permute-start(bf16[192,768]{1,0:T(8,128)(2,1)} %collective-permute-done.10), channel_id=1, source_target_pairs={{0,1},{1,2},{2,3},{3,4},{4,5},{5,6},{6,7},{7,8},{8,9},{9,10},{10,1... | collective-permute-start | bytes 884744 | tf_op jit(solution)/shard_map/ppermute | solution.py:24
  610.8 19.2 %collective-permute-start.12 = (bf16[192,768]{1,0:T(8,128)(2,1)S(1)}, bf16[192,768]{1,0:T(8,128)(2,1)S(1)}, u32[]{:S(2)}, u32[]{:S(2)}) collective-permute-start(bf16[192,768]{1,0:T(8,128)(2,1)S(1)} %collective-permute-done.11), channel_id=1, source_target_pairs={{0,1},{1,2},{2,3},{3,4},{4,5},{5,6},{6,7},{7,8},{8,9},{9,10},{10,1... | collective-permute-start | bytes 884744 | tf_op jit(solution)/shard_map/ppermute | solution.py:24
  630.0 12.2 collective-permute-start.13
  642.2 12.2 collective-permute-start.14
  668.0 349.2 %copy-start.58 = (f32[768]{0:T(1024)S(1)}, f32[768]{0:T(1024)}, u32[]{:S(2)}) copy-start(f32[768]{0:T(1024)} %get-tuple-element.62) | copy-start | bytes 9220
  669.0 494.8 %all-reduce.3.cloned.1.call-start = ((), (), s32[]{:S(2)}) async-start(), calls=%async_computation.14 | async-start | bytes 1769472 | tf_op jit(solution)/shard_map/psum | solution.py:227
  1017.2 159.6 %copy-start.47 = (f32[784]{0:T(1024)S(1)}, f32[784]{0:T(1024)}, u32[]{:S(2)}) copy-start(f32[784]{0:T(1024)} %copy-done.46) | copy-start | bytes 9412
  1017.2 159.6 %copy-start.49 = (f32[784]{0:T(1024)S(1)}, f32[784]{0:T(1024)}, u32[]{:S(2)}) copy-start(f32[784]{0:T(1024)} %copy-done.48) | copy-start | bytes 9412
  1176.9 59.0 %copy-start.16 = (f32[48,2304]{1,0:T(8,128)S(1)}, f32[48,2304]{1,0:T(8,128)}, u32[]{:S(2)}) copy-start(f32[48,2304]{1,0:T(8,128)} %param.23) | copy-start | bytes 1327108
  (57 other events, 1219.9 us)
Sparse Core Ops, SparseCore 0:
  11.4 74.1 all-gather.5
  89.0 54.6 all-gather.7
  147.1 79.3 all-gather.9
  229.7 79.0 all-gather.11
  329.6 127.0 reduce-scatter.9
  462.7 200.2 reduce-scatter.7
  669.7 170.1 reduce-scatter.11
  845.5 169.7 reduce-scatter.13
  1021.3 120.3 reduce-scatter.15
  1145.2 18.4 all-reduce.2
